TPU v7x, 32 devices: a whole 2x2x4 slice. The times are simulated.
32 devices in a mesh: energy: 4 (over z), slab: 8 (over y, x, core).
Axes of the slice: x: 2, y: 2, z: 4, core: 2. Of those that a mesh axis runs over, the one named last changes fastest.
Arguments:
- hamiltonian: float32 [2048, 256], P('slab'), as said below
- decay: float32 [8, 256], P('slab'), may hold values from 0 to 1, as said below
- coupling: float32 [8, 256], P('slab'), may hold values from 0.2 to 2
- rows: int32 [8, 32], P('slab'), may hold values from 0 to 255
- screened: float32 [8, 32, 32, 256], P('slab', None, 'energy'), may hold values from -1 to 1
Outputs:
- sigma: float32 [32, 256, 256], P('energy', 'slab')
Inputs may be any that keep to these rules, and one draw needn't show every extreme that they name: `hamiltonian`: entries are independent and small enough that every H_s / z_k has spectral radius well under one. `decay`: every entry lies strictly between 0 and 1.
All inputs are finite; a program needn't handle non-finite values.
Results may differ from a plain program's by a relative error of at most 0.0001.
Values sent between devices are 32-bit elements; how exact they have to be, the bound alone decides.
A program may use at most 128 MiB of HBM per device.

v0:
```python
import math

import jax
import jax.numpy as jnp
from jax import lax
from jax.sharding import PartitionSpec as P

E_DEV = 8
NS_ITERS = 2


FULL_PRECISION = lax.Precision.HIGHEST


def local_green(hamilton_block, shifts):
    identity = jnp.eye(hamilton_block.shape[0], dtype=jnp.float32)
    column = shifts[:, None, None]
    green_block = (identity[None] + hamilton_block[None] / column) / column
    for sweep_index in range(NS_ITERS):
        applied = jnp.einsum("ij,kjl->kil", hamilton_block, green_block, precision=FULL_PRECISION)
        shifted = column * green_block - applied
        green_block = 2.0 * green_block - jnp.einsum(
            "kij,kjl->kil", green_block, shifted, precision=FULL_PRECISION
        )
    return green_block


def transform_tables(total):
    indices = jnp.arange(total, dtype=jnp.int32)
    angles = (
        2.0 * math.pi / total * (indices[:, None] * indices[None, :] % total).astype(jnp.float32)
    )
    return (jnp.cos(angles), jnp.sin(angles))


def shards(hamiltonian, decay, coupling, rows, screened):
    energy_count = lax.axis_size("energy")
    total = E_DEV * energy_count
    slab_count = lax.axis_size("slab")
    offset_index = lax.axis_index("energy") * E_DEV
    shifts = 1.0 + (offset_index + jnp.arange(E_DEV, dtype=jnp.int32)).astype(jnp.float32) / total
    green_block = local_green(hamiltonian, shifts)
    injection_contributions = coupling * jnp.diagonal(green_block, axis1=1, axis2=2) / slab_count
    damping_rates = decay[0]
    all_rates, all_terms = (
        lax.all_gather(damping_rates[None], "slab", axis=0, tiled=True),
        lax.all_gather(injection_contributions[None], "slab", axis=0, tiled=True),
    )

    def compose(earlier, later):
        return (later[0] * earlier[0], later[0][:, None, :] * earlier[1] + later[1])

    _, prefix = lax.associative_scan(compose, (all_rates, all_terms))
    slab_place = lax.axis_index("slab")
    previous = lax.dynamic_index_in_dim(prefix, jnp.maximum(slab_place - 1, 0), 0, keepdims=False)
    incoming = jnp.where(slab_place > 0, previous, jnp.zeros_like(previous))
    picked = jnp.take(green_block, rows[0], axis=1)
    dressed = picked + jnp.einsum(
        "kri,kij->krj", picked * incoming[:, None, :], green_block, precision=FULL_PRECISION
    )
    cosine_table, sine_table = transform_tables(total)
    resident_lines = screened.shape[2]
    element_leading = lax.all_to_all(dressed, "energy", split_axis=1, concat_axis=0, tiled=True)
    flat_green = element_leading.reshape(total, -1)
    green_cos = jnp.dot(cosine_table, flat_green, precision=FULL_PRECISION)
    green_sin = jnp.dot(sine_table, flat_green, precision=FULL_PRECISION)
    flat_screen = screened[0].reshape(total, -1)
    screen_cos = jnp.dot(cosine_table, flat_screen, precision=FULL_PRECISION)
    screen_sin = jnp.dot(sine_table, flat_screen, precision=FULL_PRECISION)
    real_part = green_cos * screen_cos - green_sin * screen_sin
    imag_negated = green_cos * screen_sin + green_sin * screen_cos
    sigma_flat = (
        jnp.dot(cosine_table, real_part, precision=FULL_PRECISION)
        + jnp.dot(sine_table, imag_negated, precision=FULL_PRECISION)
    ) / total
    returned = lax.all_to_all(
        sigma_flat.reshape(total, resident_lines, -1),
        "energy",
        split_axis=0,
        concat_axis=1,
        tiled=True,
    )
    return returned


def solution(mesh):
    in_specs = (
        P("slab", None),
        P("slab", None),
        P("slab", None),
        P("slab", None),
        P("slab", None, "energy", None),
    )
    out_specs = P("energy", "slab", None)
    return jax.shard_map(shards, mesh=mesh, in_specs=in_specs, out_specs=out_specs, check_vma=False)
```

profile of v0, /device:TPU:0, one launch (start us, length us, event | category | flops | bytes accessed | tf_op | source)
XLA Modules:
  0.0 85.3 jit_solution(4185508200803909150)
XLA Ops:
  0.0 10.5 %all-gather = f32[8,1,256]{2,1,0:T(1,128)S(1)} all-gather(f32[1,1,256]{2,1,0:T(1,128)} %bitcast.82), channel_id=1, replica_groups=mesh['energy'=4,'slab'=8] {'slab'}, dimensions={0}, use_global_device_ids=true | all-gather | bytes 9216 | tf_op jit(solution)/shard_map/all_gather | solution.py:46
  10.7 1.1 %copy.30 = f32[256,256]{0,1:T(8,128)S(1)} copy(f32[256,256]{1,0:T(8,128)} %param.5) | data formatting | bytes 524288 | tf_op args[0]
  11.7 3.0 %fusion.8 = f32[8,256,256]{2,1,0:T(8,128)S(1)} fusion(f32[8]{0:T(128)S(1)} %multiply_add_fusion, f32[256,256]{0,1:T(8,128)S(1)} %copy.30, f32[256,256]{0,1:T(8,128)S(1)} %fusion.21, f32[256,256]{1,0:T(8,128)} %param.5), kind=kOutput, calls=%fused_computation.17 | convolution fusion | flops 1612185600 | bytes 2883616 | tf_op jit(solution)/shard_map/ij,kjl->kil/dot_general | solution.py:20
  14.7 3.0 %multiply_subtract_fusion.1 = f32[8,256,256]{1,2,0:T(8,128)S(1)} fusion(f32[8,256,256]{2,1,0:T(8,128)S(1)} %fusion.8, f32[8]{0:T(128)S(1)} %multiply_add_fusion, f32[256,256]{0,1:T(8,128)S(1)} %copy.30, f32[256,256]{0,1:T(8,128)S(1)} %fusion.21), kind=kOutput, calls=%fused_computation.13 | convolution fusion | flops 1617428480 | bytes 4718624 | tf_op jit(solution)/shard_map/kij,kjl->kil/dot_general | solution.py:22
  17.8 1.8 %fusion.11 = f32[8,256,256]{2,1,0:T(8,128)S(1)} fusion(f32[8,256,256]{1,2,0:T(8,128)S(1)} %multiply_subtract_fusion.1, f32[256,256]{1,0:T(8,128)S(1)} %copy-done), kind=kOutput, calls=%fused_computation.19 | convolution fusion | flops 1610612736 | bytes 4456448 | tf_op jit(solution)/shard_map/ij,kjl->kil/dot_general | solution.py:20
  19.6 2.5 %multiply_subtract_fusion = f32[8,256,256]{1,2,0:T(8,128)S(1)} fusion(f32[8,256,256]{1,2,0:T(8,128)S(1)} %multiply_subtract_fusion.1, f32[8,256,256]{2,1,0:T(8,128)S(1)} %fusion.11, f32[8]{0:T(128)S(1)} %multiply_add_fusion), kind=kOutput, calls=%fused_computation.11 | convolution fusion | flops 1612709888 | bytes 6291488 | tf_op jit(solution)/shard_map/kij,kjl->kil/dot_general | solution.py:22
  22.1 16.2 %copy.39 = f32[8,256,256]{0,2,1:T(8,128)} copy(f32[8,256,256]{1,2,0:T(8,128)S(1)} %multiply_subtract_fusion) | data formatting | bytes 4194304 | tf_op jit(solution)/shard_map/sub | solution.py:22
  38.3 2.3 %gather_fusion.1 = f32[256,8]{1,0:T(8,128)S(1)} fusion(f32[8,256,256]{0,2,1:T(8,128)} %copy.39, s32[256]{0:T(256)S(1)} %bitcast.66), kind=kCustom, calls=%fused_computation.1 | custom fusion | bytes 18432 | tf_op jit(solution)/shard_map/jit(diagonal)/gather | solution.py:43
  40.7 9.3 %all_gather.6 = f32[8,8,256]{2,1,0:T(8,128)S(1)} all-gather(f32[1,8,256]{2,1,0:T(8,128)S(1)} %fusion.37), channel_id=1, replica_groups=mesh['energy'=4,'slab'=8] {'slab'}, dimensions={0}, use_global_device_ids=true | all-gather | bytes 73728 | tf_op jit(solution)/shard_map/all_gather | solution.py:47
  50.0 2.0 %copy.37 = f32[8,256,256]{2,0,1:T(8,128)} copy(f32[8,256,256]{1,2,0:T(8,128)S(1)} %multiply_subtract_fusion) | data formatting | bytes 4194304 | tf_op jit(solution)/shard_map/sub | solution.py:22
  52.4 2.2 %gather_fusion = f32[32,8,256]{2,1,0:T(8,128)S(1)} fusion(f32[8,256,256]{2,0,1:T(8,128)} %copy.37, s32[1024]{0:T(1024)S(1)} %pad_clamp_fusion), kind=kCustom, calls=%fused_computation | custom fusion | bytes 524416 | tf_op jit(solution)/shard_map/jit(_take)/gather | solution.py:57
  54.6 2.1 %convolution_add_fusion.1 = f32[8,32,256]{2,1,0:T(8,128)S(1)} fusion(f32[8,256,256]{1,2,0:T(8,128)S(1)} %multiply_subtract_fusion, f32[32,8,256]{2,1,0:T(8,128)S(1)} %gather_fusion, f32[8,256]{1,0:T(8,128)S(1)} %fusion.36, pred[32]{0:T(512)(128)(4,1)S(1)} %compare_and_fusion), kind=kOutput, calls=%fused_computation.14 | convolution fusion | flops 201588736 | bytes 2629664 | tf_op jit(solution)/shard_map/kri,kij->krj/dot_general | solution.py:58
  56.7 0.9 %copy.42 = f32[8,32,256]{2,0,1:T(8,128)} copy(f32[8,32,256]{2,1,0:T(8,128)S(1)} %convolution_add_fusion.1) | data formatting | bytes 524288 | tf_op jit(solution)/shard_map/add | solution.py:58
  57.5 4.9 %all-to-all-start = ((f32[8,32,256]{2,0,1:T(8,128)}), f32[8,32,256]{2,0,1:T(8,128)S(1)}, u32[]{:S(2)}, u32[]{:S(2)}) async-start(f32[8,32,256]{2,0,1:T(8,128)} %copy.42), calls=%async_computation | async-start | bytes 524288 | tf_op jit(solution)/shard_map/all_to_all | solution.py:63
  62.5 0.4 fusion.41
  62.9 0.4 fusion.46
  63.4 8.4 %all-to-all-done = f32[8,32,256]{2,0,1:T(8,128)S(1)} async-done(((f32[8,32,256]{2,0,1:T(8,128)}), f32[8,32,256]{2,0,1:T(8,128)S(1)}, u32[]{:S(2)}, u32[]{:S(2)}) %all-to-all-start) | async-done | bytes 262176 | tf_op jit(solution)/shard_map/all_to_all | solution.py:63
  71.9 0.1 copy.53
  71.9 0.4 fusion.43
  72.4 0.4 fusion.48
  72.8 0.5 fusion.17
  73.3 0.5 fusion
  73.9 10.7 %all_to_all.33 = f32[32,8,256]{2,1,0:T(8,128)S(1)} all-to-all(f32[32,8,256]{2,1,0:T(8,128)S(1)} %bitcast.73), channel_id=1, replica_groups=mesh['energy'=4,'slab'=8] {'energy'}, dimensions={0} | all-to-all | bytes 524288 | tf_op jit(solution)/shard_map/all_to_all | solution.py:76
  84.6 0.7 copy.66
  (43 shorter events, 0.7 us)
Async XLA Ops:
  14.7 3.0 %copy-start = (f32[256,256]{1,0:T(8,128)S(1)}, f32[256,256]{1,0:T(8,128)}, u32[]{:S(2)}) copy-start(f32[256,256]{1,0:T(8,128)} %param.5) | copy-start | bytes 786436
  22.1 18.7 %copy-start.2 = (f32[1,256]{1,0:T(1,128)S(1)}, f32[1,256]{1,0:T(1,128)}, u32[]{:S(2)}) copy-start(f32[1,256]{1,0:T(1,128)} %param.7) | copy-start | bytes 3076
  50.0 2.0 %copy-start.3 = (s32[1,32]{1,0:T(1,128)S(1)}, s32[1,32]{1,0:T(1,128)}, u32[]{:S(2)}) copy-start(s32[1,32]{1,0:T(1,128)} %param.8) | copy-start | bytes 388
  52.3 10.1 %copy-start.1 = (f32[1,32,8,256]{3,2,1,0:T(8,128)S(1)}, f32[1,32,8,256]{3,2,1,0:T(8,128)}, u32[]{:S(2)}) copy-start(f32[1,32,8,256]{3,2,1,0:T(8,128)} %param.9) | copy-start | bytes 786436
  57.5 14.2 %all-to-all-start = ((f32[8,32,256]{2,0,1:T(8,128)}), f32[8,32,256]{2,0,1:T(8,128)S(1)}, u32[]{:S(2)}, u32[]{:S(2)}) async-start(f32[8,32,256]{2,0,1:T(8,128)} %copy.42), calls=%async_computation | async-start | bytes 524288 | tf_op jit(solution)/shard_map/all_to_all | solution.py:63
where the time goes:
time: 85.7 us; the launch traced here: 85.3 us
  blocking collectives  30.4 us (35%)
  local copies, waits for them, and re-layouts  26.1 us (30%)
  matrix products  15 us (18%)
  waiting for transfers between devices  8.39 us (10%)
  starting transfers between devices  4.87 us (6%)
    sub x2, local copies, waits for them, and re-layouts, local_green(): 2.0 * green_block  18.3 us
    all_to_all x1, blocking collectives, shards(): lax.all_to_all(sigma_flat.reshape(total, resident_lines, -1), 'energy', s...  10.7 us
    all_gather x1, blocking collectives, shards(): lax.all_gather(damping_rates[None], 'slab', axis=0, tiled=True)  10.5 us
    all_gather x1, blocking collectives, shards(): lax.all_gather(injection_contributions[None], 'slab', axis=0, tiled=True)  9.26 us
    all_to_all x1, waiting for transfers between devices, shards(): lax.all_to_all(dressed, 'energy', split_axis=1, concat_axis=0, tiled=True)  8.39 us
    dot_general x2, matrix products, local_green(): jnp.einsum('kij,kjl->kil', green_block, shifted, precision=FULL_PRECISION)  5.47 us
    all_to_all x1, starting transfers between devices, shards(): lax.all_to_all(dressed, 'energy', split_axis=1, concat_axis=0, tiled=True)  4.87 us
    dot_general x2, matrix products, local_green(): jnp.einsum('ij,kjl->kil', hamilton_block, green_block, precision=FULL_PRE...  4.8 us
  transfers between devices with their start and end apart: 1, of which 1 were waited for; matrix products, arithmetic and copies ran while one was open for 1% of the time, Pallas kernels for 0%

commit v1 on v0

v1 whole, which is shorter than its diff:
```python
import functools

import jax
import jax.numpy as jnp
from jax import lax
from jax.experimental import pallas as pl
from jax.experimental.pallas import tpu as pltpu
from jax.sharding import PartitionSpec as P

MESH = pl.DeviceIdType.MESH
POWERS = 8
SUBLANES = 8


def split(a):
    high = a.astype(jnp.bfloat16)
    return high, (a - high.astype(jnp.float32)).astype(jnp.bfloat16)


def mul(a, b):
    (a_high, a_low), (b_high, b_low) = a, b
    dot = functools.partial(jnp.dot, preferred_element_type=jnp.float32)
    return dot(a_high, b_high) + (dot(a_high, b_low) + dot(a_low, b_high))


def partner_of(place, step, count):
    if count & (count - 1):
        return lax.rem(place + step, count)
    bit = 1
    while bit <= step:
        if step & bit:
            place = place + bit - 2 * bit * lax.rem(lax.div(place, bit), 2)
        bit *= 2
    return place


def kernel(
    energies, slabs, rows_ref, decay_ref, coupling_ref, hamilton_ref, screened_ref, out_ref,
    hamilton, square, screen, dressed, sigma, decays, terms,
    in_sem, decay_send, decay_recv, term_send, term_recv, sigma_send, sigma_recv, own_sem,
):
    energy, slab = lax.axis_index("energy"), lax.axis_index("slab")
    total, lines, width = screen.shape
    share = total // energies

    barrier = pltpu.get_barrier_semaphore()
    for step in range(1, slabs):
        pl.semaphore_signal(
            barrier, inc=1, device_id=(energy, partner_of(slab, step, slabs)), device_id_type=MESH
        )
    for step in range(1, energies):
        pl.semaphore_signal(
            barrier, inc=1, device_id=(partner_of(energy, step, energies), slab), device_id_type=MESH
        )
    load_hamilton = pltpu.make_async_copy(hamilton_ref, hamilton, in_sem.at[0])
    load_screen = pltpu.make_async_copy(screened_ref, screen, in_sem.at[1])
    load_hamilton.start()
    load_screen.start()
    decays[slab] = jnp.broadcast_to(decay_ref[...], (POWERS, width))

    load_hamilton.wait()
    h1 = hamilton[...]
    t1 = h1.T
    h1s, t1s = split(h1), split(t1)
    h2 = mul(h1s, h1s)
    t2 = mul(t1s, t1s)
    h2s, t2s = split(h2), split(t2)
    h4 = mul(h2s, h2s)
    t3 = mul(t2s, t1s)
    square[...] = h2

    def trace(product):
        return jnp.sum(product, axis=0, keepdims=True)

    eye = lax.broadcasted_iota(jnp.int32, h1.shape, 0) == lax.broadcasted_iota(jnp.int32, h1.shape, 1)
    diagonals = jnp.concatenate(
        [
            jnp.ones((1, width), jnp.float32),
            trace(jnp.where(eye, h1, 0.0)),
            trace(t1 * h1),
            trace(t1 * h2),
            trace(t2 * h2),
            trace(t1 * h4),
            trace(t2 * h4),
            trace(t3 * h4),
        ],
        axis=0,
    )
    terms[slab] = diagonals * (coupling_ref[...] / slabs)

    pl.semaphore_wait(barrier, slabs + energies - 2)
    gathers = []
    for step in range(1, slabs):
        target = (energy, partner_of(slab, step, slabs))
        for held, send, recv in ((terms, term_send, term_recv), (decays, decay_send, decay_recv)):
            copy = pltpu.make_async_remote_copy(
                src_ref=held.at[slab], dst_ref=held.at[slab], send_sem=send.at[step], recv_sem=recv.at[step],
                device_id=target, device_id_type=MESH,
            )
            copy.start()
            gathers.append(copy)

    h4s = split(h4)
    lane = lax.broadcasted_iota(jnp.int32, (1, width), 1)
    chosen = [rows_ref[0, energy * lines + line] for line in range(lines)]
    v0 = jnp.concatenate([(lane == row).astype(jnp.float32) for row in chosen], axis=0)
    v1 = jnp.concatenate([hamilton[pl.ds(row, 1), :] for row in chosen], axis=0)
    v2 = jnp.concatenate([square[pl.ds(row, 1), :] for row in chosen], axis=0)
    v3 = mul(split(v1), h2s)
    lower = jnp.concatenate([v0, v1, v2, v3], axis=0)
    upper = mul(split(lower), h4s)
    v = [lower[p * lines:(p + 1) * lines] for p in range(4)] + [upper[p * lines:(p + 1) * lines] for p in range(4)]
    inverses = [1.0 / (1.0 + k / total) for k in range(total)]
    picked = []
    for inverse in inverses:
        value = v[POWERS - 1]
        for p in reversed(range(POWERS - 1)):
            value = value * inverse + v[p]
        picked.append(value * inverse)

    for copy in gathers:
        copy.wait()
    carried = jnp.zeros((POWERS, width), jnp.float32)
    for place in range(slabs - 1):
        carried = jnp.where(place < slab, decays[place] * carried + terms[place], carried)
    entering = []
    inverse_rows = 1.0 / (1.0 + lax.broadcasted_iota(jnp.int32, (total, width), 0).astype(jnp.float32) / total)
    incoming = jnp.broadcast_to(carried[POWERS - 1:], (total, width))
    for p in reversed(range(POWERS - 1)):
        incoming = incoming * inverse_rows + carried[p:p + 1]
    incoming = incoming * inverse_rows
    for k in range(total):
        entering.append(picked[k] * incoming[k:k + 1])
    u = jnp.concatenate(entering, axis=0)
    scale = 1.0 / (
        1.0 + (lax.broadcasted_iota(jnp.int32, u.shape, 0) // lines).astype(jnp.float32) / total
    )
    u = u + scale * mul(split(u), h1s)
    scale2 = scale * scale
    u = u + scale2 * mul(split(u), h2s)
    u = u + (scale2 * scale2) * mul(split(u), h4s)
    u = (jnp.concatenate(picked, axis=0) + scale * u).reshape(total, lines, width)
    dressed[pl.ds(0, total)] = u
    dressed[pl.ds(total, total)] = u

    load_screen.wait()

    def convolve(place):
        first = place * share

        def add(m, acc):
            return acc + dressed[pl.ds(total + first - m, share)] * screen[m][None]

        return lax.fori_loop(0, total, add, jnp.zeros((share, lines, width), jnp.float32), unroll=4)

    mine = pl.ds(pl.multiple_of(energy * lines, SUBLANES), lines)
    order = sorted(range(1, energies), key=lambda step: (step < energies // 2, step))
    sends = []
    for step in order:
        place = partner_of(energy, step, energies)
        sigma[step] = convolve(place)
        copy = pltpu.make_async_remote_copy(
            src_ref=sigma.at[step], dst_ref=out_ref.at[:, mine, :],
            send_sem=sigma_send.at[step], recv_sem=sigma_recv.at[step],
            device_id=(place, slab), device_id_type=MESH,
        )
        copy.start()
        sends.append(copy)
    sigma[0] = convolve(energy)
    own = pltpu.make_async_copy(sigma.at[0], out_ref.at[:, mine, :], own_sem)
    own.start()
    for copy in sends:
        copy.wait()
    own.wait()


def fused(energies, slabs, hamiltonian, decay, coupling, rows, screened):
    total, lines, width = screened.shape
    share = total // energies
    any_space, vmem = pl.BlockSpec(memory_space=pl.ANY), pl.BlockSpec(memory_space=pltpu.VMEM)
    dma = pltpu.SemaphoreType.DMA
    return pl.pallas_call(
        functools.partial(kernel, energies, slabs),
        out_shape=jax.ShapeDtypeStruct((share, lines * energies, width), jnp.float32),
        in_specs=[pl.BlockSpec(memory_space=pltpu.SMEM), vmem, vmem, any_space, any_space],
        out_specs=any_space,
        scratch_shapes=[
            pltpu.VMEM((width, width), jnp.float32),
            pltpu.VMEM((width, width), jnp.float32),
            pltpu.VMEM((total, lines, width), jnp.float32),
            pltpu.VMEM((2 * total, lines, width), jnp.float32),
            pltpu.VMEM((energies, share, lines, width), jnp.float32),
            pltpu.VMEM((slabs, POWERS, width), jnp.float32),
            pltpu.VMEM((slabs, POWERS, width), jnp.float32),
            dma((2,)),
            dma((slabs,)),
            dma((slabs,)),
            dma((slabs,)),
            dma((slabs,)),
            dma((energies,)),
            dma((energies,)),
            dma,
        ],
        compiler_params=pltpu.CompilerParams(
            collective_id=0, has_side_effects=True, vmem_limit_bytes=32 * 1024 * 1024
        ),
    )(rows, decay, coupling, hamiltonian, screened)


def unfused(energies, slabs, hamiltonian, decay, coupling, rows, screened):
    total, lines, width = screened.shape
    share = total // energies
    dot = functools.partial(jnp.dot, precision=lax.Precision.HIGHEST)
    powers = [jnp.eye(width, dtype=jnp.float32)]
    for _ in range(POWERS - 1):
        powers.append(dot(powers[-1], hamiltonian))
    powers = jnp.stack(powers)
    own = coupling * jnp.diagonal(powers, axis1=1, axis2=2) / slabs
    decays = lax.all_gather(decay, "slab", axis=0, tiled=True)
    terms = lax.all_gather(own[None], "slab", axis=0, tiled=True)
    slab = lax.axis_index("slab")

    def advance(place, carried):
        return jnp.where(place < slab, decays[place] * carried + terms[place], carried)

    carried = lax.fori_loop(0, slabs - 1, advance, jnp.zeros_like(own))
    shifts = 1.0 + jnp.arange(total, dtype=jnp.int32).astype(jnp.float32) / total
    weights = shifts[:, None] ** -(1.0 + jnp.arange(POWERS, dtype=jnp.float32))
    incoming = dot(weights, carried)
    chosen = lax.dynamic_slice_in_dim(rows[0], lax.axis_index("energy") * lines, lines)
    picked = jnp.einsum("kp,prj->krj", weights, jnp.take(powers, chosen, axis=1), precision=lax.Precision.HIGHEST)
    scale = 1.0 / shifts[:, None, None]
    u = picked * incoming[:, None, :]
    u = u + scale * dot(u, powers[1])
    u = u + scale**2 * dot(u, powers[2])
    u = u + scale**4 * dot(u, powers[4])
    dressed = picked + scale * u

    def convolve(m, acc):
        return acc + jnp.roll(dressed, m, axis=0) * screened[m][None]

    sigma = lax.fori_loop(0, total, convolve, jnp.zeros_like(dressed))
    return lax.all_to_all(sigma, "energy", split_axis=0, concat_axis=1, tiled=True)


def solution(mesh):
    energies, slabs = mesh.shape["energy"], mesh.shape["slab"]

    def shards(hamiltonian, decay, coupling, rows, screened):
        lines = screened.shape[2]
        form = unfused if lines % SUBLANES else fused
        return form(energies, slabs, hamiltonian, decay, coupling, rows, screened[0])

    in_specs = (
        P("slab", None),
        P("slab", None),
        P("slab", None),
        P("slab", None),
        P("slab", None, "energy", None),
    )
    out_specs = P("energy", "slab", None)
    return jax.shard_map(shards, mesh=mesh, in_specs=in_specs, out_specs=out_specs, check_vma=False)
```

time: 85.7 us -> 21.9 us (0.26)
  blocking collectives: 30.4 us -> 0 us
  local copies, waits for them, and re-layouts: 26.1 us -> 3.98 us
  Pallas kernels: 0 us -> 17.7 us
  matrix products: 15 us -> 0 us
  waiting for transfers between devices: 8.39 us -> 0 us
  starting transfers between devices: 4.87 us -> 0 us
    all_gather x2 -> x0, blocking collectives: 19.7 us -> none  [the longest x1 10.5 us: shards(): lax.all_gather(damping_rates[None], 'slab', axis=0, tiled=True)]
    sub x2 -> x0, local copies, waits for them, and re-layouts: 18.3 us -> none  [local_green(): 2.0 * green_block]
    pallas_call x0 -> x1, Pallas kernels: none -> 17.7 us  [fused(): pl.pallas_call(functools.partial(kernel, energies, slabs), out_shape=jax....]
    dot_general x11 -> x0, matrix products: 15 us -> none  [the longest x2 5.47 us: local_green(): jnp.einsum('kij,kjl->kil', green_block, shifted, precision=FULL_PRECISION)]
    all_to_all x1 -> x0, blocking collectives: 10.7 us -> none  [shards(): lax.all_to_all(sigma_flat.reshape(total, resident_lines, -1), 'energy', s...]
    all_to_all x1 -> x0, waiting for transfers between devices: 8.39 us -> none  [shards(): lax.all_to_all(dressed, 'energy', split_axis=1, concat_axis=0, tiled=True)]
    all_to_all x1 -> x0, starting transfers between devices: 4.87 us -> none  [shards(): lax.all_to_all(dressed, 'energy', split_axis=1, concat_axis=0, tiled=True)]
    gather x3 -> x0, local copies, waits for them, and re-layouts: 4.59 us -> none  [the longest x2 2.39 us: shards(): jnp.diagonal(green_block, axis1=1, axis2=2)]
  transfers between devices with their start and end apart: 1 -> 0, of which waited for: 1 -> 0; matrix products, arithmetic and copies ran while one was open for 1% -> 0% of each run, Pallas kernels for 0% -> 0%
where the time goes in v1:
time: 21.9 us; the launch traced here: 21.7 us
  Pallas kernels  17.7 us (81%)
  local copies, waits for them, and re-layouts  3.98 us (18%)
    pallas_call x1, Pallas kernels, fused(): pl.pallas_call(functools.partial(kernel, energies, slabs), out_shape=jax....  17.7 us
    unnamed x11, local copies, waits for them, and re-layouts  3.98 us

profile of v1, /device:TPU:0, one launch (start us, length us, event | category | flops | bytes accessed | tf_op | source)
XLA Modules:
  0.0 21.7 jit_solution(1285938354392724882)
XLA Ops:
  0.0 0.0 copy-start.4
  0.0 0.0 copy-start.2
  0.0 0.7 %copy-done.4 = s32[1,32]{1,0:T(1,128)S(1)} copy-done((s32[1,32]{1,0:T(1,128)S(1)}, s32[1,32]{1,0:T(1,128)}, u32[]{:S(2)}) %copy-start.4) | copy-done | bytes 152
  0.7 0.0 copy-done.2
  0.7 0.0 copy-start
  0.7 0.9 %copy-done = f32[256,256]{1,0:T(8,128)S(1)} copy-done((f32[256,256]{1,0:T(8,128)S(1)}, f32[256,256]{1,0:T(8,128)}, u32[]{:S(2)}) %copy-start) | copy-done | bytes 262168
  1.6 0.0 copy-start.1
  1.6 0.9 %copy-done.1 = f32[1,32,8,256]{3,2,1,0:T(8,128)S(1)} copy-done((f32[1,32,8,256]{3,2,1,0:T(8,128)S(1)}, f32[1,32,8,256]{3,2,1,0:T(8,128)}, u32[]{:S(2)}) %copy-start.1) | copy-done | bytes 262168
  2.6 0.0 copy-start.3
  2.6 0.7 %copy-done.3 = f32[1,256]{1,0:T(1,128)S(1)} copy-done((f32[1,256]{1,0:T(1,128)S(1)}, f32[1,256]{1,0:T(1,128)}, u32[]{:S(2)}) %copy-start.3) | copy-done | bytes 1048
  3.3 17.7 %shard_map.55 = f32[8,32,256]{2,1,0:T(8,128)S(1)} custom-call(s32[1,32]{1,0:T(1,128)S(1)} %copy-done.4, f32[1,256]{1,0:T(1,128)S(1)} %copy-done.2, f32[1,256]{1,0:T(1,128)S(1)} %copy-done.3, f32[256,256]{1,0:T(8,128)S(1)} %copy-done, f32[32,8,256]{2,1,0:T(8,128)S(1)} %bitcast.1), custom_call_target="tpu_custom_call" | custom-call | tf_op jit(solution)/shard_map/pallas_call | solution.py:182
  21.0 0.7 %copy.7 = f32[8,32,256]{2,1,0:T(8,128)} copy(f32[8,32,256]{2,1,0:T(8,128)S(1)} %shard_map.55) | data formatting | bytes 524288
Async XLA Ops:
  0.0 0.7 %copy-start.4 = (s32[1,32]{1,0:T(1,128)S(1)}, s32[1,32]{1,0:T(1,128)}, u32[]{:S(2)}) copy-start(s32[1,32]{1,0:T(1,128)} %rows_ref.1) | copy-start | bytes 388
  0.0 0.7 %copy-start.2 = (f32[1,256]{1,0:T(1,128)S(1)}, f32[1,256]{1,0:T(1,128)}, u32[]{:S(2)}) copy-start(f32[1,256]{1,0:T(1,128)} %decay_ref.1) | copy-start | bytes 3076
  0.7 0.9 %copy-start = (f32[256,256]{1,0:T(8,128)S(1)}, f32[256,256]{1,0:T(8,128)}, u32[]{:S(2)}) copy-start(f32[256,256]{1,0:T(8,128)} %hamilton_ref.1) | copy-start | bytes 786436
  1.6 0.9 %copy-start.1 = (f32[1,32,8,256]{3,2,1,0:T(8,128)S(1)}, f32[1,32,8,256]{3,2,1,0:T(8,128)}, u32[]{:S(2)}) copy-start(f32[1,32,8,256]{3,2,1,0:T(8,128)} %param.9) | copy-start | bytes 786436
  2.6 0.7 %copy-start.3 = (f32[1,256]{1,0:T(1,128)S(1)}, f32[1,256]{1,0:T(1,128)}, u32[]{:S(2)}) copy-start(f32[1,256]{1,0:T(1,128)} %coupling_ref.1) | copy-start | bytes 3076

commit v2 on v1

--- a/solution.py
+++ b/solution.py
@@ -24,8 +24,6 @@
 
 
 def partner_of(place, step, count):
-    if count & (count - 1):
-        return lax.rem(place + step, count)
     bit = 1
     while bit <= step:
         if step & bit:
@@ -35,27 +33,43 @@
 
 
 def kernel(
-    energies, slabs, rows_ref, decay_ref, coupling_ref, hamilton_ref, screened_ref, out_ref,
-    hamilton, square, screen, dressed, sigma, decays, terms,
+    energies, slabs, rows_hbm, decay_hbm, coupling_hbm, hamilton_ref, screened_ref, out_ref,
+    rows_ref, decay_ref, coupling_ref, hamilton, square, screen, dressed, sigma, decays, terms,
     in_sem, decay_send, decay_recv, term_send, term_recv, sigma_send, sigma_recv, own_sem,
 ):
     energy, slab = lax.axis_index("energy"), lax.axis_index("slab")
     total, lines, width = screen.shape
     share = total // energies
 
+    loads = [
+        pltpu.make_async_copy(source, held, in_sem.at[place])
+        for place, (source, held) in enumerate(
+            [
+                (hamilton_ref, hamilton),
+                (coupling_hbm, coupling_ref),
+                (decay_hbm, decay_ref),
+                (rows_hbm, rows_ref),
+                (screened_ref, screen),
+            ]
+        )
+    ]
+    for load in loads:
+        load.start()
+    load_hamilton, load_coupling, load_decay, load_rows, load_screen = loads
+
     barrier = pltpu.get_barrier_semaphore()
-    for step in range(1, slabs):
-        pl.semaphore_signal(
-            barrier, inc=1, device_id=(energy, partner_of(slab, step, slabs)), device_id_type=MESH
-        )
+    partners = [partner_of(slab, step, slabs) for step in range(1, slabs)]
+    for partner in partners:
+
+        @pl.when(partner < slab)
+        def _():
+            pl.semaphore_signal(barrier, inc=1, device_id=(energy, partner), device_id_type=MESH)
+
     for step in range(1, energies):
         pl.semaphore_signal(
             barrier, inc=1, device_id=(partner_of(energy, step, energies), slab), device_id_type=MESH
         )
-    load_hamilton = pltpu.make_async_copy(hamilton_ref, hamilton, in_sem.at[0])
-    load_screen = pltpu.make_async_copy(screened_ref, screen, in_sem.at[1])
-    load_hamilton.start()
-    load_screen.start()
+    load_decay.wait()
     decays[slab] = jnp.broadcast_to(decay_ref[...], (POWERS, width))
 
     load_hamilton.wait()
@@ -86,21 +100,29 @@
         ],
         axis=0,
     )
+    load_coupling.wait()
     terms[slab] = diagonals * (coupling_ref[...] / slabs)
 
-    pl.semaphore_wait(barrier, slabs + energies - 2)
-    gathers = []
+    pl.semaphore_wait(barrier, slabs - 1 - slab + energies - 1)
+
+    def gathers(step):
+        return [
+            pltpu.make_async_remote_copy(
+                src_ref=held.at[slab], dst_ref=held.at[slab], send_sem=send.at[step], recv_sem=recv.at[step],
+                device_id=(energy, partners[step - 1]), device_id_type=MESH,
+            )
+            for held, send, recv in ((terms, term_send, term_recv), (decays, decay_send, decay_recv))
+        ]
+
     for step in range(1, slabs):
-        target = (energy, partner_of(slab, step, slabs))
-        for held, send, recv in ((terms, term_send, term_recv), (decays, decay_send, decay_recv)):
-            copy = pltpu.make_async_remote_copy(
-                src_ref=held.at[slab], dst_ref=held.at[slab], send_sem=send.at[step], recv_sem=recv.at[step],
-                device_id=target, device_id_type=MESH,
-            )
-            copy.start()
-            gathers.append(copy)
+
+        @pl.when(partners[step - 1] > slab)
+        def _():
+            for copy in gathers(step):
+                copy.start()
 
     h4s = split(h4)
+    load_rows.wait()
     lane = lax.broadcasted_iota(jnp.int32, (1, width), 1)
     chosen = [rows_ref[0, energy * lines + line] for line in range(lines)]
     v0 = jnp.concatenate([(lane == row).astype(jnp.float32) for row in chosen], axis=0)
@@ -118,8 +140,13 @@
             value = value * inverse + v[p]
         picked.append(value * inverse)
 
-    for copy in gathers:
-        copy.wait()
+    for step in range(1, slabs):
+
+        @pl.when(partners[step - 1] < slab)
+        def _():
+            for copy in gathers(step):
+                copy.wait_recv()
+
     carried = jnp.zeros((POWERS, width), jnp.float32)
     for place in range(slabs - 1):
         carried = jnp.where(place < slab, decays[place] * carried + terms[place], carried)
@@ -172,19 +199,27 @@
     for copy in sends:
         copy.wait()
     own.wait()
+    for step in range(1, slabs):
+
+        @pl.when(partners[step - 1] > slab)
+        def _():
+            for copy in gathers(step):
+                copy.wait_send()
 
 
 def fused(energies, slabs, hamiltonian, decay, coupling, rows, screened):
     total, lines, width = screened.shape
     share = total // energies
-    any_space, vmem = pl.BlockSpec(memory_space=pl.ANY), pl.BlockSpec(memory_space=pltpu.VMEM)
     dma = pltpu.SemaphoreType.DMA
     return pl.pallas_call(
         functools.partial(kernel, energies, slabs),
         out_shape=jax.ShapeDtypeStruct((share, lines * energies, width), jnp.float32),
-        in_specs=[pl.BlockSpec(memory_space=pltpu.SMEM), vmem, vmem, any_space, any_space],
-        out_specs=any_space,
+        in_specs=[pl.BlockSpec(memory_space=pltpu.HBM)] * 5,
+        out_specs=pl.BlockSpec(memory_space=pl.ANY),
         scratch_shapes=[
+            pltpu.SMEM(rows.shape, jnp.int32),
+            pltpu.VMEM(decay.shape, jnp.float32),
+            pltpu.VMEM(coupling.shape, jnp.float32),
             pltpu.VMEM((width, width), jnp.float32),
             pltpu.VMEM((width, width), jnp.float32),
             pltpu.VMEM((total, lines, width), jnp.float32),
@@ -192,7 +227,7 @@
             pltpu.VMEM((energies, share, lines, width), jnp.float32),
             pltpu.VMEM((slabs, POWERS, width), jnp.float32),
             pltpu.VMEM((slabs, POWERS, width), jnp.float32),
-            dma((2,)),
+            dma((5,)),
             dma((slabs,)),
             dma((slabs,)),
             dma((slabs,)),
@@ -202,7 +237,7 @@
             dma,
         ],
         compiler_params=pltpu.CompilerParams(
-            collective_id=0, has_side_effects=True, vmem_limit_bytes=32 * 1024 * 1024
+            collective_id=0, has_side_effects=True, vmem_limit_bytes=60 * 1024 * 1024
         ),
     )(rows, decay, coupling, hamiltonian, screened)
 
@@ -248,7 +283,8 @@
 
     def shards(hamiltonian, decay, coupling, rows, screened):
         lines = screened.shape[2]
-        form = unfused if lines % SUBLANES else fused
+        fits = lines % SUBLANES == 0 and all(count & (count - 1) == 0 for count in (energies, slabs))
+        form = fused if fits else unfused
         return form(energies, slabs, hamiltonian, decay, coupling, rows, screened[0])
 
     in_specs = (

time: 21.9 us -> 17 us (0.78)
  the two profiles are of different devices: /device:TPU:0 before, /device:TPU:4 now
where the time goes in v2:
time: 17 us; the launch traced here: 16.8 us
  Pallas kernels  15.1 us (89%)
  local copies, waits for them, and re-layouts  1.67 us (10%)
    pallas_call x1, Pallas kernels, fused(): pl.pallas_call(functools.partial(kernel, energies, slabs), out_shape=jax....  15.1 us
    unnamed x1, local copies, waits for them, and re-layouts  1.67 us

profile of v2, /device:TPU:4, one launch (start us, length us, event | category | flops | bytes accessed | tf_op | source)
XLA Modules:
  0.0 16.8 jit_solution(9410439753558376499)
XLA Ops:
  0.0 15.1 %shard_map.55 = f32[8,32,256]{2,1,0:T(8,128)} custom-call(s32[1,32]{1,0:T(1,128)} %rows_hbm.1, f32[1,256]{1,0:T(1,128)} %decay_hbm.1, f32[1,256]{1,0:T(1,128)} %coupling_hbm.1, f32[256,256]{1,0:T(8,128)} %hamilton_ref.1, f32[32,8,256]{2,1,0:T(8,128)} %bitcast.1), custom_call_target="tpu_custom_call" | custom-call | tf_op jit(solution)/shard_map/pallas_call | solution.py:214
  15.1 1.7 %copy.7 = f32[8,32,256]{2,1,0:T(8,128)} copy(f32[8,32,256]{2,1,0:T(8,128)} %shard_map.55) | data formatting | bytes 524288

commit v3 on v2

--- a/solution.py
+++ b/solution.py
@@ -35,7 +35,7 @@
 def kernel(
     energies, slabs, rows_hbm, decay_hbm, coupling_hbm, hamilton_ref, screened_ref, out_ref,
     rows_ref, decay_ref, coupling_ref, hamilton, square, screen, dressed, sigma, decays, terms,
-    in_sem, decay_send, decay_recv, term_send, term_recv, sigma_send, sigma_recv, own_sem,
+    in_sem, decay_send, decay_recv, term_send, term_recv, sigma_send, sigma_recv,
 ):
     energy, slab = lax.axis_index("energy"), lax.axis_index("slab")
     total, lines, width = screen.shape
@@ -108,10 +108,13 @@
     def gathers(step):
         return [
             pltpu.make_async_remote_copy(
-                src_ref=held.at[slab], dst_ref=held.at[slab], send_sem=send.at[step], recv_sem=recv.at[step],
+                src_ref=held.at[slab, taken], dst_ref=held.at[slab, taken], send_sem=send.at[step], recv_sem=recv.at[step],
                 device_id=(energy, partners[step - 1]), device_id_type=MESH,
             )
-            for held, send, recv in ((terms, term_send, term_recv), (decays, decay_send, decay_recv))
+            for held, taken, send, recv in (
+                (terms, pl.ds(0, POWERS), term_send, term_recv),
+                (decays, pl.ds(0, 1), decay_send, decay_recv),
+            )
         ]
 
     for step in range(1, slabs):
@@ -149,7 +152,7 @@
 
     carried = jnp.zeros((POWERS, width), jnp.float32)
     for place in range(slabs - 1):
-        carried = jnp.where(place < slab, decays[place] * carried + terms[place], carried)
+        carried = jnp.where(place < slab, decays[place, 0:1] * carried + terms[place], carried)
     entering = []
     inverse_rows = 1.0 / (1.0 + lax.broadcasted_iota(jnp.int32, (total, width), 0).astype(jnp.float32) / total)
     incoming = jnp.broadcast_to(carried[POWERS - 1:], (total, width))
@@ -193,12 +196,9 @@
         )
         copy.start()
         sends.append(copy)
-    sigma[0] = convolve(energy)
-    own = pltpu.make_async_copy(sigma.at[0], out_ref.at[:, mine, :], own_sem)
-    own.start()
+    out_ref[:, mine, :] = convolve(energy)
     for copy in sends:
         copy.wait()
-    own.wait()
     for step in range(1, slabs):
 
         @pl.when(partners[step - 1] > slab)
@@ -213,9 +213,9 @@
     dma = pltpu.SemaphoreType.DMA
     return pl.pallas_call(
         functools.partial(kernel, energies, slabs),
-        out_shape=jax.ShapeDtypeStruct((share, lines * energies, width), jnp.float32),
+        out_shape=pltpu.VMEM((share, lines * energies, width), jnp.float32),
         in_specs=[pl.BlockSpec(memory_space=pltpu.HBM)] * 5,
-        out_specs=pl.BlockSpec(memory_space=pl.ANY),
+        out_specs=pl.BlockSpec(memory_space=pltpu.VMEM),
         scratch_shapes=[
             pltpu.SMEM(rows.shape, jnp.int32),
             pltpu.VMEM(decay.shape, jnp.float32),
@@ -234,7 +234,6 @@
             dma((slabs,)),
             dma((energies,)),
             dma((energies,)),
-            dma,
         ],
         compiler_params=pltpu.CompilerParams(
             collective_id=0, has_side_effects=True, vmem_limit_bytes=60 * 1024 * 1024

time: 17 us -> 15.5 us (0.912)
  local copies, waits for them, and re-layouts: 1.67 us -> 0.71 us
  Pallas kernels: 15.1 us -> 14.7 us
    unnamed x1, local copies, waits for them, and re-layouts: 1.67 us -> 0.71 us
    pallas_call x1, Pallas kernels: 15.1 us -> 14.7 us  [fused(): pl.pallas_call(functools.partial(kernel, energies, slabs), out_shape=pltp...]
where the time goes in v3:
time: 15.5 us; the launch traced here: 15.4 us
  Pallas kernels  14.7 us (95%)
  local copies, waits for them, and re-layouts  0.71 us (5%)
    pallas_call x1, Pallas kernels, fused(): pl.pallas_call(functools.partial(kernel, energies, slabs), out_shape=pltp...  14.7 us
    unnamed x1, local copies, waits for them, and re-layouts  0.71 us

profile of v3, /device:TPU:4, one launch (start us, length us, event | category | flops | bytes accessed | tf_op | source)
XLA Modules:
  0.0 15.4 jit_solution(12786439533882627515)
XLA Ops:
  0.0 14.7 %shard_map.55 = f32[8,32,256]{2,1,0:T(8,128)S(1)} custom-call(s32[1,32]{1,0:T(1,128)} %rows_hbm.1, f32[1,256]{1,0:T(1,128)} %decay_hbm.1, f32[1,256]{1,0:T(1,128)} %coupling_hbm.1, f32[256,256]{1,0:T(8,128)} %hamilton_ref.1, f32[32,8,256]{2,1,0:T(8,128)} %bitcast.1), custom_call_target="tpu_custom_call" | custom-call | tf_op jit(solution)/shard_map/pallas_call | solution.py:214
  14.7 0.7 %copy.7 = f32[8,32,256]{2,1,0:T(8,128)} copy(f32[8,32,256]{2,1,0:T(8,128)S(1)} %shard_map.55) | data formatting | bytes 524288

commit v4 on v3

--- a/solution.py
+++ b/solution.py
@@ -10,6 +10,7 @@
 MESH = pl.DeviceIdType.MESH
 POWERS = 8
 SUBLANES = 8
+EARLY = 1
 
 
 def split(a):
@@ -34,8 +35,8 @@
 
 def kernel(
     energies, slabs, rows_hbm, decay_hbm, coupling_hbm, hamilton_ref, screened_ref, out_ref,
-    rows_ref, decay_ref, coupling_ref, hamilton, square, screen, dressed, sigma, decays, terms,
-    in_sem, decay_send, decay_recv, term_send, term_recv, sigma_send, sigma_recv,
+    rows_ref, decay_ref, coupling_ref, hamilton, square, screen, early, dressed, sigma, arrived, decays, terms,
+    in_sem, decay_send, decay_recv, term_send, term_recv, sigma_send, sigma_recv, early_send, early_recv,
 ):
     energy, slab = lax.axis_index("energy"), lax.axis_index("slab")
     total, lines, width = screen.shape
@@ -124,24 +125,40 @@
             for copy in gathers(step):
                 copy.start()
 
+    kept = lines - EARLY
+    shares = []
+    for step in range(1, energies):
+        copy = pltpu.make_async_remote_copy(
+            src_ref=screened_ref.at[:, pl.ds(kept, EARLY), :], dst_ref=early.at[energy, :, pl.ds(kept, EARLY), :],
+            send_sem=early_send.at[step], recv_sem=early_recv.at[step],
+            device_id=(partner_of(energy, step, energies), slab), device_id_type=MESH,
+        )
+        copy.start()
+        shares.append(copy)
+
     h4s = split(h4)
+    lane = lax.broadcasted_iota(jnp.int32, (1, width), 1)
+    inverses = [1.0 / (1.0 + k / total) for k in range(total)]
     load_rows.wait()
-    lane = lax.broadcasted_iota(jnp.int32, (1, width), 1)
-    chosen = [rows_ref[0, energy * lines + line] for line in range(lines)]
-    v0 = jnp.concatenate([(lane == row).astype(jnp.float32) for row in chosen], axis=0)
-    v1 = jnp.concatenate([hamilton[pl.ds(row, 1), :] for row in chosen], axis=0)
-    v2 = jnp.concatenate([square[pl.ds(row, 1), :] for row in chosen], axis=0)
-    v3 = mul(split(v1), h2s)
-    lower = jnp.concatenate([v0, v1, v2, v3], axis=0)
-    upper = mul(split(lower), h4s)
-    v = [lower[p * lines:(p + 1) * lines] for p in range(4)] + [upper[p * lines:(p + 1) * lines] for p in range(4)]
-    inverses = [1.0 / (1.0 + k / total) for k in range(total)]
-    picked = []
-    for inverse in inverses:
-        value = v[POWERS - 1]
-        for p in reversed(range(POWERS - 1)):
-            value = value * inverse + v[p]
-        picked.append(value * inverse)
+
+    def pick(places):
+        chosen = [rows_ref[0, place] for place in places]
+        v0 = jnp.concatenate([(lane == row).astype(jnp.float32) for row in chosen], axis=0)
+        v1 = jnp.concatenate([hamilton[pl.ds(row, 1), :] for row in chosen], axis=0)
+        v2 = jnp.concatenate([square[pl.ds(row, 1), :] for row in chosen], axis=0)
+        v3 = mul(split(v1), h2s)
+        lower = jnp.concatenate([v0, v1, v2, v3], axis=0)
+        upper = mul(split(lower), h4s)
+        v = [part[p * lines:(p + 1) * lines] for part in (lower, upper) for p in range(POWERS // 2)]
+        picked = []
+        for inverse in inverses:
+            value = v[POWERS - 1]
+            for p in reversed(range(POWERS - 1)):
+                value = value * inverse + v[p]
+            picked.append(value * inverse)
+        return picked
+
+    picked = pick([energy * lines + line for line in range(lines)])
 
     for step in range(1, slabs):
 
@@ -153,52 +170,76 @@
     carried = jnp.zeros((POWERS, width), jnp.float32)
     for place in range(slabs - 1):
         carried = jnp.where(place < slab, decays[place, 0:1] * carried + terms[place], carried)
-    entering = []
     inverse_rows = 1.0 / (1.0 + lax.broadcasted_iota(jnp.int32, (total, width), 0).astype(jnp.float32) / total)
     incoming = jnp.broadcast_to(carried[POWERS - 1:], (total, width))
     for p in reversed(range(POWERS - 1)):
         incoming = incoming * inverse_rows + carried[p:p + 1]
     incoming = incoming * inverse_rows
-    for k in range(total):
-        entering.append(picked[k] * incoming[k:k + 1])
-    u = jnp.concatenate(entering, axis=0)
     scale = 1.0 / (
-        1.0 + (lax.broadcasted_iota(jnp.int32, u.shape, 0) // lines).astype(jnp.float32) / total
+        1.0 + (lax.broadcasted_iota(jnp.int32, (total * lines, width), 0) // lines).astype(jnp.float32) / total
     )
-    u = u + scale * mul(split(u), h1s)
     scale2 = scale * scale
-    u = u + scale2 * mul(split(u), h2s)
-    u = u + (scale2 * scale2) * mul(split(u), h4s)
-    u = (jnp.concatenate(picked, axis=0) + scale * u).reshape(total, lines, width)
-    dressed[pl.ds(0, total)] = u
-    dressed[pl.ds(total, total)] = u
-
+
+    def dress(picked):
+        u = jnp.concatenate([picked[k] * incoming[k:k + 1] for k in range(total)], axis=0)
+        u = u + scale * mul(split(u), h1s)
+        u = u + scale2 * mul(split(u), h2s)
+        u = u + (scale2 * scale2) * mul(split(u), h4s)
+        u = (jnp.concatenate(picked, axis=0) + scale * u).reshape(total, lines, width)
+        dressed[pl.ds(0, total)] = u
+        dressed[pl.ds(total, total)] = u
+
+    def convolve(place, held):
+        first = place * share
+
+        def add(m, acc):
+            return acc + dressed[pl.ds(total + first - m, share)] * held[m][None]
+
+        return lax.fori_loop(0, total, add, jnp.zeros((share, lines, width), jnp.float32), unroll=4)
+
+    dress(picked)
     load_screen.wait()
 
-    def convolve(place):
-        first = place * share
-
-        def add(m, acc):
-            return acc + dressed[pl.ds(total + first - m, share)] * screen[m][None]
-
-        return lax.fori_loop(0, total, add, jnp.zeros((share, lines, width), jnp.float32), unroll=4)
-
-    mine = pl.ds(pl.multiple_of(energy * lines, SUBLANES), lines)
+    def pack(block):
+        fill = jnp.concatenate(
+            [jnp.zeros((kept, kept, width), jnp.float32)] + [block[k, :kept][:, None] for k in range(kept, share)], axis=1
+        )
+        line = lax.broadcasted_iota(jnp.int32, fill.shape, 1)
+        return jnp.where(line < kept, block[:kept], fill)
+
     order = sorted(range(1, energies), key=lambda step: (step < energies // 2, step))
     sends = []
     for step in order:
         place = partner_of(energy, step, energies)
-        sigma[step] = convolve(place)
+        sigma[step] = pack(convolve(place, screen))
         copy = pltpu.make_async_remote_copy(
-            src_ref=sigma.at[step], dst_ref=out_ref.at[:, mine, :],
+            src_ref=sigma.at[step], dst_ref=arrived.at[energy],
             send_sem=sigma_send.at[step], recv_sem=sigma_recv.at[step],
             device_id=(place, slab), device_id_type=MESH,
         )
         copy.start()
         sends.append(copy)
-    out_ref[:, mine, :] = convolve(energy)
+    arrived[energy] = pack(convolve(energy, screen))
+
+    places = [place * lines + kept + line for place in range(energies) for line in range(EARLY)]
+    dress(pick(places + [places[-1]] * (lines - len(places))))
+    early[energy, :, pl.ds(kept, EARLY), :] = screen[:, kept:]
+    for copy in shares:
+        copy.wait()
+    parts = [early[place, :, pl.ds(kept, EARLY), :] for place in range(energies)]
+    parts += [jnp.zeros((total, lines - len(places), width), jnp.float32)] * (len(places) < lines)
+    screen[...] = jnp.concatenate(parts, axis=1)
+    result = convolve(energy, screen)
+    for place in range(energies):
+        out_ref[:, pl.ds(place * lines + kept, EARLY), :] = result[:, place * EARLY:(place + 1) * EARLY]
+
     for copy in sends:
         copy.wait()
+    for place in range(energies):
+        first = place * lines
+        out_ref[:kept, first:first + kept] = arrived[place, :, :kept]
+        for k in range(kept, share):
+            out_ref[k, first:first + kept] = arrived[place, :, k]
     for step in range(1, slabs):
 
         @pl.when(partners[step - 1] > slab)
@@ -223,8 +264,10 @@
             pltpu.VMEM((width, width), jnp.float32),
             pltpu.VMEM((width, width), jnp.float32),
             pltpu.VMEM((total, lines, width), jnp.float32),
+            pltpu.VMEM((energies, total, lines, width), jnp.float32),
             pltpu.VMEM((2 * total, lines, width), jnp.float32),
-            pltpu.VMEM((energies, share, lines, width), jnp.float32),
+            pltpu.VMEM((energies, share - EARLY, lines, width), jnp.float32),
+            pltpu.VMEM((energies, share - EARLY, lines, width), jnp.float32),
             pltpu.VMEM((slabs, POWERS, width), jnp.float32),
             pltpu.VMEM((slabs, POWERS, width), jnp.float32),
             dma((5,)),
@@ -232,6 +275,8 @@
             dma((slabs,)),
             dma((slabs,)),
             dma((slabs,)),
+            dma((energies,)),
+            dma((energies,)),
             dma((energies,)),
             dma((energies,)),
         ],
@@ -282,7 +327,7 @@
 
     def shards(hamiltonian, decay, coupling, rows, screened):
         lines = screened.shape[2]
-        fits = lines % SUBLANES == 0 and all(count & (count - 1) == 0 for count in (energies, slabs))
+        fits = lines == screened.shape[1] // energies == SUBLANES >= energies * EARLY and all(count & (count - 1) == 0 for count in (energies, slabs))
         form = fused if fits else unfused
         return form(energies, slabs, hamiltonian, decay, coupling, rows, screened[0])
 

time: 15.5 us -> 15.8 us (1.019)
  the two profiles are of different devices: /device:TPU:4 before, /device:TPU:0 now
where the time goes in v4:
time: 15.8 us; the launch traced here: 15.7 us
  Pallas kernels  15 us (95%)
  local copies, waits for them, and re-layouts  0.71 us (4%)
    pallas_call x1, Pallas kernels, fused(): pl.pallas_call(functools.partial(kernel, energies, slabs), out_shape=pltp...  15 us
    unnamed x1, local copies, waits for them, and re-layouts  0.71 us

profile of v4, /device:TPU:0, one launch (start us, length us, event | category | flops | bytes accessed | tf_op | source)
XLA Modules:
  0.0 15.7 jit_solution(5688327663372561022)
XLA Ops:
  0.0 15.0 %shard_map.55 = f32[8,32,256]{2,1,0:T(8,128)S(1)} custom-call(s32[1,32]{1,0:T(1,128)} %rows_hbm.1, f32[1,256]{1,0:T(1,128)} %decay_hbm.1, f32[1,256]{1,0:T(1,128)} %coupling_hbm.1, f32[256,256]{1,0:T(8,128)} %hamilton_ref.1, f32[32,8,256]{2,1,0:T(8,128)} %bitcast.1), custom_call_target="tpu_custom_call" | custom-call | tf_op jit(solution)/shard_map/pallas_call | solution.py:255
  15.0 0.7 %copy.7 = f32[8,32,256]{2,1,0:T(8,128)} copy(f32[8,32,256]{2,1,0:T(8,128)S(1)} %shard_map.55) | data formatting | bytes 524288

commit v5 on v4

--- a/solution.py
+++ b/solution.py
@@ -207,16 +207,19 @@
         line = lax.broadcasted_iota(jnp.int32, fill.shape, 1)
         return jnp.where(line < kept, block[:kept], fill)
 
-    order = sorted(range(1, energies), key=lambda step: (step < energies // 2, step))
+
+    def deliver(slot, source, target):
+        return pltpu.make_async_remote_copy(
+            src_ref=sigma.at[slot], dst_ref=arrived.at[source],
+            send_sem=sigma_send.at[slot], recv_sem=sigma_recv.at[source],
+            device_id=(target, slab), device_id_type=MESH,
+        )
+
     sends = []
-    for step in order:
-        place = partner_of(energy, step, energies)
-        sigma[step] = pack(convolve(place, screen))
-        copy = pltpu.make_async_remote_copy(
-            src_ref=sigma.at[step], dst_ref=arrived.at[energy],
-            send_sem=sigma_send.at[step], recv_sem=sigma_recv.at[step],
-            device_id=(place, slab), device_id_type=MESH,
-        )
+    for slot in range(energies - 1):
+        place = slot + (slot >= energy).astype(jnp.int32)
+        sigma[slot] = pack(convolve(place, screen))
+        copy = deliver(slot, energy, place)
         copy.start()
         sends.append(copy)
     arrived[energy] = pack(convolve(energy, screen))
@@ -233,8 +236,9 @@
     for place in range(energies):
         out_ref[:, pl.ds(place * lines + kept, EARLY), :] = result[:, place * EARLY:(place + 1) * EARLY]
 
-    for copy in sends:
-        copy.wait()
+    for slot, copy in enumerate(sends):
+        copy.wait_send()
+        deliver(slot, slot + (slot >= energy).astype(jnp.int32), energy).wait_recv()
     for place in range(energies):
         first = place * lines
         out_ref[:kept, first:first + kept] = arrived[place, :, :kept]

time: 15.8 us -> 15.8 us (level)
  no operation moved by 1% of the time
where the time goes in v5:
time: 15.8 us; the launch traced here: 15.7 us
  Pallas kernels  14.9 us (94%)
  local copies, waits for them, and re-layouts  0.71 us (4%)
    pallas_call x1, Pallas kernels, fused(): pl.pallas_call(functools.partial(kernel, energies, slabs), out_shape=pltp...  14.9 us
    unnamed x1, local copies, waits for them, and re-layouts  0.71 us

profile of v5, /device:TPU:0, one launch (start us, length us, event | category | flops | bytes accessed | tf_op | source)
XLA Modules:
  0.0 15.7 jit_solution(1105921982669860372)
XLA Ops:
  0.0 14.9 %shard_map.55 = f32[8,32,256]{2,1,0:T(8,128)S(1)} custom-call(s32[1,32]{1,0:T(1,128)} %rows_hbm.1, f32[1,256]{1,0:T(1,128)} %decay_hbm.1, f32[1,256]{1,0:T(1,128)} %coupling_hbm.1, f32[256,256]{1,0:T(8,128)} %hamilton_ref.1, f32[32,8,256]{2,1,0:T(8,128)} %bitcast.1), custom_call_target="tpu_custom_call" | custom-call | tf_op jit(solution)/shard_map/pallas_call | solution.py:259
  15.0 0.7 %copy.7 = f32[8,32,256]{2,1,0:T(8,128)} copy(f32[8,32,256]{2,1,0:T(8,128)S(1)} %shard_map.55) | data formatting | bytes 524288

commit v6 on v5

--- a/solution.py
+++ b/solution.py
@@ -20,8 +20,9 @@
 
 def mul(a, b):
     (a_high, a_low), (b_high, b_low) = a, b
-    dot = functools.partial(jnp.dot, preferred_element_type=jnp.float32)
-    return dot(a_high, b_high) + (dot(a_high, b_low) + dot(a_low, b_high))
+    left = jnp.concatenate([a_low, a_high, a_high], axis=1)
+    right = jnp.concatenate([b_high, b_low, b_high], axis=0)
+    return jnp.dot(left, right, preferred_element_type=jnp.float32)
 
 
 def partner_of(place, step, count):
@@ -78,7 +79,7 @@
     t1 = h1.T
     h1s, t1s = split(h1), split(t1)
     h2 = mul(h1s, h1s)
-    t2 = mul(t1s, t1s)
+    t2 = h2.T
     h2s, t2s = split(h2), split(t2)
     h4 = mul(h2s, h2s)
     t3 = mul(t2s, t1s)
@@ -181,13 +182,24 @@
     scale2 = scale * scale
 
     def dress(picked):
-        u = jnp.concatenate([picked[k] * incoming[k:k + 1] for k in range(total)], axis=0)
-        u = u + scale * mul(split(u), h1s)
-        u = u + scale2 * mul(split(u), h2s)
-        u = u + (scale2 * scale2) * mul(split(u), h4s)
-        u = (jnp.concatenate(picked, axis=0) + scale * u).reshape(total, lines, width)
-        dressed[pl.ds(0, total)] = u
-        dressed[pl.ds(total, total)] = u
+        bare = jnp.concatenate(picked, axis=0)
+
+        def store(value):
+            value = value.reshape(total, lines, width)
+            dressed[pl.ds(0, total)] = value
+            dressed[pl.ds(total, total)] = value
+
+        @pl.when(slab == 0)
+        def _():
+            store(bare)
+
+        @pl.when(slab > 0)
+        def _():
+            u = jnp.concatenate([picked[k] * incoming[k:k + 1] for k in range(total)], axis=0)
+            u = u + scale * mul(split(u), h1s)
+            u = u + scale2 * mul(split(u), h2s)
+            u = u + (scale2 * scale2) * mul(split(u), h4s)
+            store(bare + scale * u)
 
     def convolve(place, held):
         first = place * share

time: 15.8 us -> 15.5 us (0.981)
  Pallas kernels: 14.9 us -> 14.6 us
    pallas_call x1, Pallas kernels: 14.9 us -> 14.6 us  [fused(): pl.pallas_call(functools.partial(kernel, energies, slabs), out_shape=pltp...]
where the time goes in v6:
time: 15.5 us; the launch traced here: 15.3 us
  Pallas kernels  14.6 us (94%)
  local copies, waits for them, and re-layouts  0.71 us (5%)
    pallas_call x1, Pallas kernels, fused(): pl.pallas_call(functools.partial(kernel, energies, slabs), out_shape=pltp...  14.6 us
    unnamed x1, local copies, waits for them, and re-layouts  0.71 us

profile of v6, /device:TPU:0, one launch (start us, length us, event | category | flops | bytes accessed | tf_op | source)
XLA Modules:
  0.0 15.3 jit_solution(15395058155970772355)
XLA Ops:
  0.0 14.6 %shard_map.55 = f32[8,32,256]{2,1,0:T(8,128)S(1)} custom-call(s32[1,32]{1,0:T(1,128)} %rows_hbm.1, f32[1,256]{1,0:T(1,128)} %decay_hbm.1, f32[1,256]{1,0:T(1,128)} %coupling_hbm.1, f32[256,256]{1,0:T(8,128)} %hamilton_ref.1, f32[32,8,256]{2,1,0:T(8,128)} %bitcast.1), custom_call_target="tpu_custom_call" | custom-call | tf_op jit(solution)/shard_map/pallas_call | solution.py:271
  14.6 0.7 %copy.7 = f32[8,32,256]{2,1,0:T(8,128)} copy(f32[8,32,256]{2,1,0:T(8,128)S(1)} %shard_map.55) | data formatting | bytes 524288

commit v7 on v6

--- a/solution.py
+++ b/solution.py
@@ -10,7 +10,6 @@
 MESH = pl.DeviceIdType.MESH
 POWERS = 8
 SUBLANES = 8
-EARLY = 1
 
 
 def split(a):
@@ -36,8 +35,8 @@
 
 def kernel(
     energies, slabs, rows_hbm, decay_hbm, coupling_hbm, hamilton_ref, screened_ref, out_ref,
-    rows_ref, decay_ref, coupling_ref, hamilton, square, screen, early, dressed, sigma, arrived, decays, terms,
-    in_sem, decay_send, decay_recv, term_send, term_recv, sigma_send, sigma_recv, early_send, early_recv,
+    rows_ref, decay_ref, coupling_ref, hamilton, square, screen, dressed, sigma, decays, terms,
+    in_sem, decay_send, decay_recv, term_send, term_recv, sigma_send, sigma_recv,
 ):
     energy, slab = lax.axis_index("energy"), lax.axis_index("slab")
     total, lines, width = screen.shape
@@ -126,17 +125,6 @@
             for copy in gathers(step):
                 copy.start()
 
-    kept = lines - EARLY
-    shares = []
-    for step in range(1, energies):
-        copy = pltpu.make_async_remote_copy(
-            src_ref=screened_ref.at[:, pl.ds(kept, EARLY), :], dst_ref=early.at[energy, :, pl.ds(kept, EARLY), :],
-            send_sem=early_send.at[step], recv_sem=early_recv.at[step],
-            device_id=(partner_of(energy, step, energies), slab), device_id_type=MESH,
-        )
-        copy.start()
-        shares.append(copy)
-
     h4s = split(h4)
     lane = lax.broadcasted_iota(jnp.int32, (1, width), 1)
     inverses = [1.0 / (1.0 + k / total) for k in range(total)]
@@ -212,17 +200,12 @@
     dress(picked)
     load_screen.wait()
 
-    def pack(block):
-        fill = jnp.concatenate(
-            [jnp.zeros((kept, kept, width), jnp.float32)] + [block[k, :kept][:, None] for k in range(kept, share)], axis=1
-        )
-        line = lax.broadcasted_iota(jnp.int32, fill.shape, 1)
-        return jnp.where(line < kept, block[:kept], fill)
-
+    def lines_of(place):
+        return pl.ds(pl.multiple_of(place * lines, SUBLANES), lines)
 
     def deliver(slot, source, target):
         return pltpu.make_async_remote_copy(
-            src_ref=sigma.at[slot], dst_ref=arrived.at[source],
+            src_ref=sigma.at[slot], dst_ref=out_ref.at[:, lines_of(source), :],
             send_sem=sigma_send.at[slot], recv_sem=sigma_recv.at[source],
             device_id=(target, slab), device_id_type=MESH,
         )
@@ -230,32 +213,15 @@
     sends = []
     for slot in range(energies - 1):
         place = slot + (slot >= energy).astype(jnp.int32)
-        sigma[slot] = pack(convolve(place, screen))
+        sigma[slot] = convolve(place, screen)
         copy = deliver(slot, energy, place)
         copy.start()
         sends.append(copy)
-    arrived[energy] = pack(convolve(energy, screen))
-
-    places = [place * lines + kept + line for place in range(energies) for line in range(EARLY)]
-    dress(pick(places + [places[-1]] * (lines - len(places))))
-    early[energy, :, pl.ds(kept, EARLY), :] = screen[:, kept:]
-    for copy in shares:
-        copy.wait()
-    parts = [early[place, :, pl.ds(kept, EARLY), :] for place in range(energies)]
-    parts += [jnp.zeros((total, lines - len(places), width), jnp.float32)] * (len(places) < lines)
-    screen[...] = jnp.concatenate(parts, axis=1)
-    result = convolve(energy, screen)
-    for place in range(energies):
-        out_ref[:, pl.ds(place * lines + kept, EARLY), :] = result[:, place * EARLY:(place + 1) * EARLY]
+    out_ref[:, lines_of(energy), :] = convolve(energy, screen)
 
     for slot, copy in enumerate(sends):
         copy.wait_send()
         deliver(slot, slot + (slot >= energy).astype(jnp.int32), energy).wait_recv()
-    for place in range(energies):
-        first = place * lines
-        out_ref[:kept, first:first + kept] = arrived[place, :, :kept]
-        for k in range(kept, share):
-            out_ref[k, first:first + kept] = arrived[place, :, k]
     for step in range(1, slabs):
 
         @pl.when(partners[step - 1] > slab)
@@ -280,10 +246,8 @@
             pltpu.VMEM((width, width), jnp.float32),
             pltpu.VMEM((width, width), jnp.float32),
             pltpu.VMEM((total, lines, width), jnp.float32),
-            pltpu.VMEM((energies, total, lines, width), jnp.float32),
             pltpu.VMEM((2 * total, lines, width), jnp.float32),
-            pltpu.VMEM((energies, share - EARLY, lines, width), jnp.float32),
-            pltpu.VMEM((energies, share - EARLY, lines, width), jnp.float32),
+            pltpu.VMEM((energies - 1, share, lines, width), jnp.float32),
             pltpu.VMEM((slabs, POWERS, width), jnp.float32),
             pltpu.VMEM((slabs, POWERS, width), jnp.float32),
             dma((5,)),
@@ -291,8 +255,6 @@
             dma((slabs,)),
             dma((slabs,)),
             dma((slabs,)),
-            dma((energies,)),
-            dma((energies,)),
             dma((energies,)),
             dma((energies,)),
         ],
@@ -343,7 +305,7 @@
 
     def shards(hamiltonian, decay, coupling, rows, screened):
         lines = screened.shape[2]
-        fits = lines == screened.shape[1] // energies == SUBLANES >= energies * EARLY and all(count & (count - 1) == 0 for count in (energies, slabs))
+        fits = lines % SUBLANES == 0 and all(count & (count - 1) == 0 for count in (energies, slabs))
         form = fused if fits else unfused
         return form(energies, slabs, hamiltonian, decay, coupling, rows, screened[0])
 

time: 15.5 us -> 15.4 us (level)
  the two profiles are of different devices: /device:TPU:0 before, /device:TPU:4 now
where the time goes in v7:
time: 15.4 us; the launch traced here: 15.3 us
  Pallas kernels  14.6 us (95%)
  local copies, waits for them, and re-layouts  0.71 us (5%)
    pallas_call x1, Pallas kernels, fused(): pl.pallas_call(functools.partial(kernel, energies, slabs), out_shape=pltp...  14.6 us
    unnamed x1, local copies, waits for them, and re-layouts  0.71 us

profile of v7, /device:TPU:4, one launch (start us, length us, event | category | flops | bytes accessed | tf_op | source)
XLA Modules:
  0.0 15.3 jit_solution(8483440699989672980)
XLA Ops:
  0.0 14.6 %shard_map.55 = f32[8,32,256]{2,1,0:T(8,128)S(1)} custom-call(s32[1,32]{1,0:T(1,128)} %rows_hbm.1, f32[1,256]{1,0:T(1,128)} %decay_hbm.1, f32[1,256]{1,0:T(1,128)} %coupling_hbm.1, f32[256,256]{1,0:T(8,128)} %hamilton_ref.1, f32[32,8,256]{2,1,0:T(8,128)} %bitcast.1), custom_call_target="tpu_custom_call" | custom-call | tf_op jit(solution)/shard_map/pallas_call | solution.py:237
  14.6 0.7 %copy.7 = f32[8,32,256]{2,1,0:T(8,128)} copy(f32[8,32,256]{2,1,0:T(8,128)S(1)} %shard_map.55) | data formatting | bytes 524288

commit v8 on v7

--- a/solution.py
+++ b/solution.py
@@ -118,12 +118,12 @@
             )
         ]
 
-    for step in range(1, slabs):
-
-        @pl.when(partners[step - 1] > slab)
-        def _():
-            for copy in gathers(step):
-                copy.start()
+    for kind in range(2):
+        for step in range(1, slabs):
+
+            @pl.when(partners[step - 1] > slab)
+            def _():
+                gathers(step)[kind].start()
 
     h4s = split(h4)
     lane = lax.broadcasted_iota(jnp.int32, (1, width), 1)

time: 15.4 us -> 15.5 us (level)
  the two profiles are of different devices: /device:TPU:4 before, /device:TPU:2 now
where the time goes in v8:
time: 15.5 us; the launch traced here: 15.3 us
  Pallas kernels  14.6 us (94%)
  local copies, waits for them, and re-layouts  0.71 us (5%)
    pallas_call x1, Pallas kernels, fused(): pl.pallas_call(functools.partial(kernel, energies, slabs), out_shape=pltp...  14.6 us
    unnamed x1, local copies, waits for them, and re-layouts  0.71 us

profile of v8, /device:TPU:2, one launch (start us, length us, event | category | flops | bytes accessed | tf_op | source)
XLA Modules:
  0.0 15.3 jit_solution(17992933170679802919)
XLA Ops:
  0.0 14.6 %shard_map.55 = f32[8,32,256]{2,1,0:T(8,128)S(1)} custom-call(s32[1,32]{1,0:T(1,128)} %rows_hbm.1, f32[1,256]{1,0:T(1,128)} %decay_hbm.1, f32[1,256]{1,0:T(1,128)} %coupling_hbm.1, f32[256,256]{1,0:T(8,128)} %hamilton_ref.1, f32[32,8,256]{2,1,0:T(8,128)} %bitcast.1), custom_call_target="tpu_custom_call" | custom-call | tf_op jit(solution)/shard_map/pallas_call | solution.py:237
  14.6 0.7 %copy.7 = f32[8,32,256]{2,1,0:T(8,128)} copy(f32[8,32,256]{2,1,0:T(8,128)S(1)} %shard_map.55) | data formatting | bytes 524288
